TPU v7x, 128 devices: a whole 4x4x4 slice. The times are simulated.
128 devices in a mesh: node: 16 (over z, y_hi, core), local: 8 (over y_lo, x).
Axes of the slice: x: 4, y: 4 (y_hi: 2, y_lo: 2; y = y_hi * 2 + y_lo), z: 4, core: 2. Of those that a mesh axis runs over, the one named last changes fastest.
Arguments:
- tokens: bfloat16 [32768, 14336], P(('node', 'local')), may hold values from -24 to 24
- cotangent: bfloat16 [32768, 384], P(('node', 'local')), may hold values from -12 to 12
- master: float32 [384, 14336], P('local', 'node'), may hold values from -0.046875 to 0.046875
- moment_one: float32 [384, 14336], P('local', 'node'), may hold values from -6 to 6
- moment_two: float32 [384, 14336], P('local', 'node'), may hold values from 0.5 to 8
Outputs:
- hidden: bfloat16 [32768, 384], P(('node', 'local'))
- input_grad: bfloat16 [32768, 14336], P(('node', 'local'))
- gradient: float32 [384, 14336], P('local', 'node')
- master_new: float32 [384, 14336], P('local', 'node')
- moment_one_new: float32 [384, 14336], P('local', 'node')
- moment_two_new: float32 [384, 14336], P('local', 'node')
All inputs are finite; a program needn't handle non-finite values.
Results may differ from a plain program's by a relative error of at most 0.022.
Values may be sent and summed in bfloat16 or wider, within the bound.
A program may use at most 128 MiB of HBM per device.

v0:
```python
import jax
import jax.numpy as jnp
from jax import lax
from jax.sharding import PartitionSpec as P

STEP = 10


beta_one = 0.9
beta_two = 0.95
learn_rate = 0.001
adam_eps = 1e-08
gelu_coef = 0.7978845608
gelu_cube = 0.044715


def gelu_value(pre_act):
    tanh_val = jnp.tanh(gelu_coef * (pre_act + gelu_cube * pre_act * pre_act * pre_act))
    return 0.5 * pre_act * (1.0 + tanh_val)


def gelu_slope(pre_act):
    tanh_val = jnp.tanh(gelu_coef * (pre_act + gelu_cube * pre_act * pre_act * pre_act))
    inner = gelu_coef * (1.0 + 3.0 * gelu_cube * pre_act * pre_act)
    return 0.5 * (1.0 + tanh_val) + 0.5 * pre_act * (1.0 - tanh_val * tanh_val) * inner


def project_units(weight_rows, tokens):
    return lax.dot_general(
        weight_rows, tokens, (((1,), (1,)), ((), ())), preferred_element_type=jnp.float32
    )


def units_to_width(unit_grad, weight_rows):
    return lax.dot_general(
        unit_grad, weight_rows, (((0,), (0,)), ((), ())), preferred_element_type=jnp.float32
    )


def shards(tokens, cotangent, master, moment_one, moment_two):
    weight_bf = master.astype(jnp.bfloat16)
    secondary = lax.all_gather(weight_bf, "node", axis=1, tiled=True)
    cot_units = cotangent.T
    pre_units = project_units(lax.all_gather(secondary, "local", axis=0, tiled=True), tokens)
    hidden = gelu_value(pre_units).T.astype(jnp.bfloat16)
    weight_rows = lax.all_gather(secondary, "local", axis=0, tiled=True)
    pre_piece = project_units(weight_rows, tokens)
    piece_grad = (cot_units.astype(jnp.float32) * gelu_slope(pre_piece)).astype(jnp.bfloat16)
    running = units_to_width(piece_grad, weight_rows)
    input_grad = running.astype(jnp.bfloat16)
    product = jnp.dot(piece_grad, tokens, preferred_element_type=jnp.float32)
    in_group = lax.psum_scatter(
        product.astype(jnp.bfloat16).astype(jnp.float32).astype(jnp.bfloat16),
        "local",
        scatter_dimension=0,
        tiled=True,
    )
    summed = lax.psum_scatter(in_group, "node", scatter_dimension=1, tiled=True).astype(jnp.float32)
    gradient = summed / (lax.axis_size("node") * lax.axis_size("local"))
    moment_one_new = beta_one * moment_one + (1.0 - beta_one) * gradient
    moment_two_new = beta_two * moment_two + (1.0 - beta_two) * gradient * gradient
    first_fix = 1.0 - beta_one**STEP
    second_fix = 1.0 - beta_two**STEP
    master_new = master - learn_rate * (moment_one_new / first_fix) / (
        jnp.sqrt(moment_two_new / second_fix) + adam_eps
    )
    return (hidden, input_grad, gradient, master_new, moment_one_new, moment_two_new)


def solution(mesh):
    in_specs = (
        P(("node", "local"), None),
        P(("node", "local"), None),
        P("local", "node"),
        P("local", "node"),
        P("local", "node"),
    )
    out_specs = (
        P(("node", "local"), None),
        P(("node", "local"), None),
        P("local", "node"),
        P("local", "node"),
        P("local", "node"),
        P("local", "node"),
    )
    return jax.shard_map(shards, mesh=mesh, in_specs=in_specs, out_specs=out_specs, check_vma=False)
```

profile of v0, /device:TPU:0, one launch (start us, length us, event | category | flops | bytes accessed | tf_op | source)
XLA Modules:
  0.0 401.2 jit_solution(10943460908943152055)
XLA Ops:
  7.2 0.0 all-gather.3.cloned.1.call-start
  7.2 1.6 convert_element_type.26
  8.8 0.0 all-gather.3.cloned.1.call-update
  8.8 0.0 all-gather.5.cloned.1.call-start
  8.9 50.6 %all-gather.3.cloned.1.call-done = bf16[48,14336]{1,0:T(8,128)(2,1)} async-done(((bf16[48,896]{1,0:T(8,128)(2,1)}), bf16[48,14336]{1,0:T(8,128)(2,1)}) %all-gather.3.cloned.1.call-update) | async-done | bytes 1376272 | tf_op jit(solution)/shard_map/all_gather | solution.py:42
  59.5 0.0 all-gather.5.cloned.1.call-update
  59.5 0.0 reduce-scatter.5.cloned.1.call-start
  59.6 1.1 copy.13
  60.6 115.7 %all-gather.5.cloned.1.call-done = bf16[384,14336]{1,0:T(8,128)(2,1)} async-done(((bf16[48,14336]{1,0:T(8,128)(2,1)}), bf16[384,14336]{1,0:T(8,128)(2,1)}) %all-gather.5.cloned.1.call-update) | async-done | bytes 11010064 | tf_op jit(solution)/shard_map/all_gather | solution.py:44
  176.3 9.9 %fusion.4 = (bf16[256,384]{0,1:T(8,128)(2,1)S(1)}, f32[384,256]{1,0:T(8,128)S(1)}) fusion(bf16[384,14336]{1,0:T(8,128)(2,1)} %all-gather.5.cloned.1.call-done, bf16[256,14336]{1,0:T(8,128)(2,1)} %param.5), kind=kOutput, calls=%fused_computation.9 | convolution fusion | flops 2819457024 | bytes 18939904 | tf_op jit(solution)/shard_map/dot_general | solution.py:29
  186.3 8.9 %convolution_convert_fusion = bf16[384,14336]{1,0:T(8,128)(2,1)} fusion(bf16[256,14336]{1,0:T(8,128)(2,1)} %param.5, f32[384,256]{1,0:T(8,128)S(1)} %get-tuple-element.23, bf16[256,384]{0,1:T(8,128)(2,1)S(1)} %copy.13), kind=kOutput, calls=%fused_computation | convolution fusion | flops 2826043392 | bytes 18939904 | tf_op jit(solution)/shard_map/dot_general | solution.py:51
  195.1 0.0 reduce-scatter.5.cloned.1.call-update
  195.1 0.0 reduce-scatter.7.cloned.1.call-start
  195.2 116.3 %reduce-scatter.5.cloned.1.call-done = bf16[48,14336]{1,0:T(8,128)(2,1)} async-done(((bf16[384,14336]{1,0:T(8,128)(2,1)}), bf16[48,14336]{1,0:T(8,128)(2,1)}) %reduce-scatter.5.cloned.1.call-update) | async-done | bytes 1376272 | tf_op jit(solution)/shard_map/reduce_scatter | solution.py:52
  311.5 4.4 %copy.15 = bf16[48,14336]{0,1:T(8,128)(2,1)} copy(bf16[48,14336]{1,0:T(8,128)(2,1)} %reduce-scatter.5.cloned.1.call-done) | data formatting | bytes 2752512
  315.9 0.0 reduce-scatter.7.cloned.1.call-update
  316.0 0.8 copy.14
  316.8 10.5 %convolution_convert_fusion.1 = bf16[256,14336]{1,0:T(8,128)(2,1)} fusion(bf16[384,14336]{1,0:T(8,128)(2,1)} %all-gather.5.cloned.1.call-done, f32[384,256]{1,0:T(8,128)S(1)} %get-tuple-element.23, bf16[256,384]{0,1:T(8,128)(2,1)S(1)} %copy.13), kind=kOutput, calls=%fused_computation.1 | convolution fusion | flops 2824208384 | bytes 18939904 | tf_op jit(solution)/shard_map/dot_general | solution.py:35
  327.3 65.3 %reduce-scatter.7.cloned.1.call-done = bf16[896,48]{1,0:T(8,128)(2,1)} async-done(((bf16[14336,48]{1,0:T(8,128)(2,1)}), bf16[896,48]{1,0:T(8,128)(2,1)}) %reduce-scatter.7.cloned.1.call-update) | async-done | bytes 86032
  392.6 1.1 copy.16
  393.7 0.0 copy-done
  393.7 0.0 copy-done.1
  393.7 0.0 copy-done.2
  393.7 0.9 divide_subtract_fusion
  (3 shorter events, 0.0 us)
Async XLA Ops:
  7.2 52.3 %all-gather.3.cloned.1.call-start = ((), (), s32[]{:S(2)}) async-start(), calls=%async_computation.2 | async-start | bytes 1462272 | tf_op jit(solution)/shard_map/all_gather | solution.py:42
  8.8 167.5 %all-gather.5.cloned.1.call-start = ((), (), s32[]{:S(2)}) async-start(), calls=%async_computation.3 | async-start | bytes 12386304 | tf_op jit(solution)/shard_map/all_gather | solution.py:44
  59.5 252.0 %reduce-scatter.5.cloned.1.call-start = ((), (), s32[]{:S(2)}) async-start(), calls=%async_computation.4 | async-start | bytes 12386304 | tf_op jit(solution)/shard_map/reduce_scatter | solution.py:52
  195.1 197.5 %reduce-scatter.7.cloned.1.call-start = ((), (), s32[]{:S(2)}) async-start(), calls=%async_computation.5 | async-start | bytes 3899392
  316.8 76.9 %copy-start = (f32[48,896]{1,0:T(8,128)S(1)}, f32[48,896]{1,0:T(8,128)}, u32[]{:S(2)}) copy-start(f32[48,896]{1,0:T(8,128)} %param.7) | copy-start | bytes 516100
  316.8 76.9 %copy-start.1 = (f32[48,896]{1,0:T(8,128)S(1)}, f32[48,896]{1,0:T(8,128)}, u32[]{:S(2)}) copy-start(f32[48,896]{1,0:T(8,128)} %param.8) | copy-start | bytes 516100
  316.8 76.9 %copy-start.2 = (f32[48,896]{1,0:T(8,128)S(1)}, f32[48,896]{1,0:T(8,128)}, u32[]{:S(2)}) copy-start(f32[48,896]{1,0:T(8,128)} %param.9) | copy-start | bytes 516100
Sparse Core Ops, SparseCore 0:
  10.9 48.5 all-gather.2
  61.1 115.1 all-gather.4
  195.3 116.1 reduce-scatter.4
  316.1 76.5 reduce-scatter.6
where the time goes:
time: 401 us
  waiting for transfers between devices  348 us (87%)
  matrix products  29.3 us (7%)
  between operations  13.8 us (3%)
  local copies, waits for them, and re-layouts  7.39 us (2%)
    reduce_scatter x1, waiting for transfers between devices, shards(): lax.psum_scatter(product.astype(jnp.bfloat16).astype(jnp.float32).astype(...  116 us
    all_gather x1, waiting for transfers between devices, shards(): lax.all_gather(secondary, 'local', axis=0, tiled=True)  116 us
    unnamed x5, waiting for transfers between devices  65.4 us
    all_gather x1, waiting for transfers between devices, shards(): secondary = lax.all_gather(weight_bf, 'node', axis=1, tiled=True)  50.6 us
    dot_general x1, matrix products, units_to_width(): lax.dot_general(unit_grad, weight_rows, (((0,), (0,)), ((), ())), preferr...  10.5 us
    dot_general x1, matrix products, project_units(): lax.dot_general(weight_rows, tokens, (((1,), (1,)), ((), ())), preferred_...  9.94 us
    dot_general x1, matrix products, shards(): product = jnp.dot(piece_grad, tokens, preferred_element_type=jnp.float32)  8.85 us
  transfers between devices with their start and end apart: 4, of which 4 were waited for; matrix products, arithmetic and copies ran while one was open for 3% of the time, Pallas kernels for 0%

commit v1 on v0

v1 whole, which is shorter than its diff:
```python
import functools

import jax
import jax.numpy as jnp
from jax import lax
from jax.experimental import pallas as pl
from jax.experimental.pallas import tpu as pltpu
from jax.sharding import PartitionSpec as P

MESH = pl.DeviceIdType.MESH
STEP = 10

beta_one = 0.9
beta_two = 0.95
learn_rate = 0.001
adam_eps = 1e-08
gelu_coef = 0.7978845608
gelu_cube = 0.044715

ORDERS = (("x", "y", "z"), ("y", "z", "x"), ("z", "x", "y"))
ROWS = 16
PARTS = 3


def wrap(value):
    return lax.rem(value + 4, 4)


def flip(value):
    return value + 1 - 2 * lax.rem(value, 2)


def device(at, core):
    node = at["z"] * 4 + (at["y"] // 2) * 2 + core
    local = lax.rem(at["y"], 2) * 4 + at["x"]
    return (node, local)


def kernel(
    master, tokens, cot, out_grad, out_hidden, out_input,
    weights, tok, terms, acc, pre_in, act_t, act, cot_t, stage, hop_a, hop_b, hop_c, row_a, row_b, row_c, last_in,
    tok_sem, tok_send, tok_recv, pre_send, pre_recv, act_send, act_recv, in_send, in_recv,
    ag_send, ag_recv, rs_send, rs_recv,
):
    node, local = lax.axis_index("node"), lax.axis_index("local")
    core = lax.rem(node, 2)
    me = {"x": lax.rem(local, 4), "y": lax.rem(node // 2, 2) * 2 + local // 4, "z": node // 4}
    sign = 1 - 2 * core
    width = master.shape[1]
    half = tokens.shape[0]

    def near(dim, step):
        at = dict(me)
        at[dim] = wrap(at[dim] + step)
        return device(at, core)

    partner = device(me, 1 - core)
    around = [near(dim, step) for dim in "xyz" for step in (1, 3, 2)] + [partner]
    barrier = pltpu.get_barrier_semaphore()
    for other in around:
        pl.semaphore_signal(barrier, inc=1, device_id=other, device_id_type=MESH)

    own_tok = [
        pltpu.make_async_copy(
            tokens.at[:, pl.ds(pl.multiple_of((2 * k + core) * width, 128), width)],
            tok.at[k, pl.ds(pl.multiple_of(core * half, half), half), :],
            tok_sem.at[k],
        )
        for k in range(8)
    ]
    for copy in own_tok:
        copy.start()
    weights[me["z"], me["y"], me["x"]] = master[...].astype(jnp.bfloat16)
    pl.semaphore_wait(barrier, len(around))

    sent = []

    def send(src, dst, send_sem, recv_sem, to):
        copy = pltpu.make_async_remote_copy(
            src_ref=src, dst_ref=dst, send_sem=send_sem, recv_sem=recv_sem, device_id=to, device_id_type=MESH
        )
        copy.start()
        sent.append(copy)

    def arrived(dst, send_sem, recv_sem):
        pltpu.make_async_remote_copy(
            src_ref=dst, dst_ref=dst, send_sem=send_sem, recv_sem=recv_sem, device_id=partner, device_id_type=MESH
        ).wait_recv()

    def block(buf, part, place):
        return buf.at[
            tuple(pl.ds(0, 4) if place[d] is None else place[d] for d in "zyx")
            + (pl.ds(part * ROWS, ROWS), slice(None))
        ]

    def ag(part, msg, src_place, to):
        region = block(weights, part, src_place)
        send(region, region, ag_send.at[part, msg], ag_recv.at[part, msg], to)

    def ag_wait(part, msg, place):
        arrived(block(weights, part, place), ag_send.at[part, msg], ag_recv.at[part, msg])

    for i, step in enumerate((1, 3, 2)):
        for part, (one, two, three) in enumerate(ORDERS):
            ag(part, i, me, near(one, step))
    for k in range(8):
        send(
            tokens.at[:, pl.ds(pl.multiple_of((2 * k + 1 - core) * width, 128), width)],
            tok.at[k, pl.ds(pl.multiple_of(core * half, half), half), :],
            tok_send.at[k],
            tok_recv.at[k],
            partner,
        )
    cot_t[...] = cot[...].astype(jnp.float32).T.astype(jnp.bfloat16)
    for i, step in enumerate((1, 3, 2)):
        for part, (one, two, three) in enumerate(ORDERS):
            ag_wait(part, i, {**me, one: wrap(me[one] - step)})

    def rows_of(dim):
        return (me[dim], wrap(me[dim] - sign), wrap(me[dim] + sign), wrap(me[dim] + 2))

    def row(part, which, plane):
        one, two, three = ORDERS[part]
        return {one: None, two: rows_of(two)[which], three: rows_of(three)[plane]}

    def second(part, which):
        two = ORDERS[part][1]
        if which == 2:
            ag(part, 5, row(part, 1, 0), near(two, sign))
        else:
            ag(part, 3 + which, row(part, 0, 0), near(two, sign if which == 0 else -sign))

    def third(part, which, kind):
        three = ORDERS[part][2]
        if kind == 2:
            ag(part, 6 + 3 * which + 2, row(part, which, 1), near(three, sign))
        else:
            ag(part, 6 + 3 * which + kind, row(part, which, 0), near(three, sign if kind == 0 else -sign))

    def third_wait(part, which, kind):
        ag_wait(part, 6 + 3 * which + kind, row(part, which, kind + 1))

    every = range(PARTS)
    for part in every:
        second(part, 0)
        second(part, 1)
    for part in every:
        third(part, 0, 0)
        third(part, 0, 1)
    for part in every:
        ag_wait(part, 3, row(part, 1, 0))
        second(part, 2)
        third(part, 1, 0)
        third(part, 1, 1)
    for part in every:
        ag_wait(part, 4, row(part, 2, 0))
        third(part, 2, 0)
        third(part, 2, 1)
    for part in every:
        third_wait(part, 0, 0)
        third(part, 0, 2)
    for part in every:
        ag_wait(part, 5, row(part, 3, 0))
        third(part, 3, 0)
        third(part, 3, 1)
    for which in (1, 2, 3):
        for part in every:
            third_wait(part, which, 0)
            third(part, which, 2)
    acc[...] = jnp.zeros_like(acc)
    for k in range(8):
        own_tok[k].wait()
        arrived(
            tok.at[k, pl.ds(pl.multiple_of((1 - core) * half, half), half), :], tok_send.at[k], tok_recv.at[k]
        )
    for which in range(4):
        for part in every:
            third_wait(part, which, 1)
    for which in range(4):
        for part in every:
            third_wait(part, which, 2)

    def chunk_of(buf, z, upper):
        units = 8 * PARTS * ROWS
        return buf[z, pl.ds(2 * upper, 2)].reshape(units, width)

    def forward(k, carry):
        acc[...] += lax.dot_general(
            chunk_of(weights, k // 2, lax.rem(k, 2)), tok[k], (((1,), (1,)), ((), ())),
            preferred_element_type=jnp.float32,
        )
        return carry

    lax.fori_loop(0, 8, forward, 0)

    mine = pl.ds(pl.multiple_of(core * half, half), half)
    theirs = pl.ds(pl.multiple_of((1 - core) * half, half), half)
    send(acc.at[:, theirs], pre_in, pre_send, pre_recv, partner)
    arrived(pre_in, pre_send, pre_recv)
    pre = acc[:, mine] + pre_in[...]
    tanh_val = jnp.tanh(gelu_coef * (pre + gelu_cube * pre * pre * pre))
    inner = gelu_coef * (1.0 + 3.0 * gelu_cube * pre * pre)
    slope = 0.5 * (1.0 + tanh_val) + 0.5 * pre * (1.0 - tanh_val * tanh_val) * inner
    act_t[:, mine] = (cot_t[...].astype(jnp.float32) * slope).astype(jnp.bfloat16)
    send(act_t.at[:, mine], act_t.at[:, mine], act_send, act_recv, partner)
    out_hidden[...] = (0.5 * pre * (1.0 + tanh_val)).T.astype(jnp.bfloat16)
    arrived(act_t.at[:, theirs], act_send, act_recv)

    def term(z, upper):
        value = jnp.dot(act_t[...], tok[2 * z + upper], preferred_element_type=jnp.float32)
        terms[z, pl.ds(2 * upper, 2)] = value.astype(jnp.bfloat16).reshape(2, 4, PARTS * ROWS, width)

    def order(dim):
        far = wrap(me[dim] + 2)
        return (far, flip(far), flip(me[dim]), me[dim])

    def term_row(part, which, plane):
        one, two, three = ORDERS[part]
        return block(terms, part, {one: None, two: order(two)[which], three: wrap(me[three] + plane)})

    def rs(part, msg, src, dst, to):
        send(src, dst, rs_send.at[part, msg], rs_recv.at[part, msg], to)

    def rs_wait(part, msg, dst):
        arrived(dst, rs_send.at[part, msg], rs_recv.at[part, msg])

    def far_send(part, which):
        rs(part, which, term_row(part, which, 2), hop_a.at[part, which], near(ORDERS[part][2], sign))

    def back_send(part, which):
        rs(part, 8 + which, term_row(part, which, -sign), hop_c.at[part, which], near(ORDERS[part][2], -sign))

    def sum_into(dst, *terms_in):
        total = terms_in[0][...].astype(jnp.float32)
        for value in terms_in[1:]:
            total += value[...].astype(jnp.float32)
        dst[...] = total.astype(dst.dtype)

    up = me["y"] // 2
    zs = (wrap(me["z"] + 2), wrap(me["z"] - sign), wrap(me["z"] + sign), me["z"])
    for upper_is_far in (1, 0):
        upper = 1 - up if upper_is_far else up
        for i, z in enumerate(zs):
            term(z, upper)
            if i == 0:
                for which in (0, 1) if upper_is_far else (2, 3):
                    far_send(0, which)
            if i == 1:
                for which in (0, 1) if upper_is_far else (2, 3):
                    back_send(0, which)
            if not upper_is_far:
                which = {0: 0, 3: 3}.get(i)
                if which is not None:
                    far_send(1, which)
                    back_send(1, which)
                if i == 2:
                    for which in (1, 2):
                        far_send(1, which)
                        back_send(1, which)
        if upper_is_far:
            for which in range(4):
                far_send(2, which)
    for which in range(4):
        back_send(2, which)

    act[...] = act_t[...].astype(jnp.float32).T.astype(jnp.bfloat16)

    def input_chunk(k):
        z, upper = k // 2, k % 2
        weight = chunk_of(weights, z, upper)
        columns = pl.ds(pl.multiple_of((2 * k + core) * width, 128), width)
        stage[k] = jnp.dot(act[theirs, :], weight, preferred_element_type=jnp.float32).astype(jnp.bfloat16)
        send(stage.at[k], out_input.at[:, columns], in_send.at[k], in_recv.at[k], partner)
        out_input[:, columns] = jnp.dot(act[mine, :], weight, preferred_element_type=jnp.float32).astype(
            jnp.bfloat16
        )

    for k in range(2):
        input_chunk(k)
    for which in range(4):
        for part in every:
            rs_wait(part, which, hop_a.at[part, which])
            sum_into(hop_a.at[part, which], hop_a.at[part, which], term_row(part, which, sign))
            rs(part, 4 + which, hop_a.at[part, which], hop_b.at[part, which], near(ORDERS[part][2], sign))
        input_chunk(2 + which)

    def second_row(part, plane):
        one, two, three = ORDERS[part]
        return block(terms, part, {one: None, two: wrap(me[two] + plane), three: me[three]})

    for which in range(4):
        for part in every:
            rs_wait(part, 4 + which, hop_b.at[part, which])
            rs_wait(part, 8 + which, hop_c.at[part, which])
            here = term_row(part, which, 0)
            sum_into(here, here, hop_b.at[part, which], hop_c.at[part, which])
        for part in every:
            two = ORDERS[part][1]
            if which == 0:
                rs(part, 12, second_row(part, 2), row_a.at[part], near(two, sign))
            if which == 2:
                rs(part, 14, second_row(part, -sign), row_c.at[part], near(two, -sign))
        if which == 2:
            for part in every:
                rs_wait(part, 12, row_a.at[part])
                sum_into(row_a.at[part], row_a.at[part], second_row(part, sign))
                rs(part, 13, row_a.at[part], row_b.at[part], near(ORDERS[part][1], sign))
            input_chunk(6)
            input_chunk(7)

    for part in every:
        rs_wait(part, 13, row_b.at[part])
        rs_wait(part, 14, row_c.at[part])
        here = second_row(part, 0)
        sum_into(here, here, row_b.at[part], row_c.at[part])
        one = ORDERS[part][0]
        for i, step in enumerate((2, 1, 3)):
            rs(
                part, 15 + i, block(terms, part, {**me, one: wrap(me[one] + step)}), last_in.at[part, i],
                near(one, step),
            )
    for part in every:
        for i in range(3):
            rs_wait(part, 15 + i, last_in.at[part, i])
        sum_into(
            out_grad.at[pl.ds(part * ROWS, ROWS), :], block(terms, part, me), *(last_in.at[part, i] for i in range(3))
        )

    for k in range(8):
        arrived(
            out_input.at[:, pl.ds(pl.multiple_of((2 * k + 1 - core) * width, 128), width)], in_send.at[k], in_recv.at[k]
        )
    for copy in sent:
        copy.wait_send()


def shards(tokens, cotangent, master, moment_one, moment_two):
    half, model = tokens.shape
    units, width = master.shape
    all_units = cotangent.shape[1]
    bf, f32 = jnp.bfloat16, jnp.float32
    dma = pltpu.SemaphoreType.DMA
    vmem = pl.BlockSpec(memory_space=pltpu.VMEM)
    total, hidden, input_grad = pl.pallas_call(
        kernel,
        out_shape=(
            jax.ShapeDtypeStruct((units, width), f32),
            jax.ShapeDtypeStruct((half, all_units), bf),
            jax.ShapeDtypeStruct((half, model), bf),
        ),
        in_specs=[vmem, pl.BlockSpec(memory_space=pl.ANY), vmem],
        out_specs=(vmem, vmem, vmem),
        scratch_shapes=[
            pltpu.VMEM((4, 4, 4, units, width), bf),
            pltpu.VMEM((8, 2 * half, width), bf),
            pltpu.VMEM((4, 4, 4, units, width), bf),
            pltpu.VMEM((all_units, 2 * half), f32),
            pltpu.VMEM((all_units, half), f32),
            pltpu.VMEM((all_units, 2 * half), bf),
            pltpu.VMEM((2 * half, all_units), bf),
            pltpu.VMEM((all_units, half), bf),
            pltpu.VMEM((8, half, width), bf),
            pltpu.VMEM((PARTS, 4, 4, ROWS, width), bf),
            pltpu.VMEM((PARTS, 4, 4, ROWS, width), bf),
            pltpu.VMEM((PARTS, 4, 4, ROWS, width), bf),
            pltpu.VMEM((PARTS, 4, ROWS, width), bf),
            pltpu.VMEM((PARTS, 4, ROWS, width), bf),
            pltpu.VMEM((PARTS, 4, ROWS, width), bf),
            pltpu.VMEM((PARTS, 3, ROWS, width), bf),
            dma((8,)), dma((8,)), dma((8,)), dma, dma, dma, dma, dma((8,)), dma((8,)),
            dma((PARTS, 18)), dma((PARTS, 18)), dma((PARTS, 18)), dma((PARTS, 18)),
        ],
        compiler_params=pltpu.CompilerParams(
            collective_id=0, has_side_effects=True, vmem_limit_bytes=56 * 2**20
        ),
        name="gather_project_scatter",
    )(master, tokens, cotangent)
    gradient = total / (lax.axis_size("node") * lax.axis_size("local"))
    moment_one_new = beta_one * moment_one + (1.0 - beta_one) * gradient
    moment_two_new = beta_two * moment_two + (1.0 - beta_two) * gradient * gradient
    first_fix = 1.0 - beta_one**STEP
    second_fix = 1.0 - beta_two**STEP
    master_new = master - learn_rate * (moment_one_new / first_fix) / (
        jnp.sqrt(moment_two_new / second_fix) + adam_eps
    )
    return (hidden, input_grad, gradient, master_new, moment_one_new, moment_two_new)


def solution(mesh):
    in_specs = (
        P(("node", "local"), None),
        P(("node", "local"), None),
        P("local", "node"),
        P("local", "node"),
        P("local", "node"),
    )
    out_specs = (
        P(("node", "local"), None),
        P(("node", "local"), None),
        P("local", "node"),
        P("local", "node"),
        P("local", "node"),
        P("local", "node"),
    )
    return jax.shard_map(shards, mesh=mesh, in_specs=in_specs, out_specs=out_specs, check_vma=False)
```

time: 401 us -> 87.9 us (0.22)
  waiting for transfers between devices: 348 us -> 0 us
  Pallas kernels: 0 us -> 76.7 us
  matrix products: 29.3 us -> 0 us
  between operations: 13.8 us -> 0.69 us
    all_gather x2 -> x0, waiting for transfers between devices: 166 us -> none  [the longest x1 116 us: shards(): lax.all_gather(secondary, 'local', axis=0, tiled=True)]
    reduce_scatter x1 -> x0, waiting for transfers between devices: 116 us -> none  [shards(): lax.psum_scatter(product.astype(jnp.bfloat16).astype(jnp.float32).astype(...]
    pallas_call x0 -> x1, Pallas kernels: none -> 76.7 us  [shards(): pl.pallas_call(kernel, out_shape=(jax.ShapeDtypeStruct((units, width), f3...]
    unnamed x5 -> x0, waiting for transfers between devices: 65.4 us -> none
    dot_general x3 -> x0, matrix products: 29.3 us -> none  [the longest x1 10.5 us: units_to_width(): lax.dot_general(unit_grad, weight_rows, (((0,), (0,)), ((), ())), preferr...]
    unnamed x10 -> x8, local copies, waits for them, and re-layouts: 7.39 us -> 8.53 us
  transfers between devices with their start and end apart: 4 -> 0, of which waited for: 4 -> 0; matrix products, arithmetic and copies ran while one was open for 3% -> 0% of each run, Pallas kernels for 0% -> 0%
where the time goes in v1:
time: 87.9 us; the launch traced here: 87.7 us
  Pallas kernels  76.7 us (87%)
  local copies, waits for them, and re-layouts  8.53 us (10%)
  other arithmetic  1.83 us (2%)
    pallas_call x1, Pallas kernels, shards(): pl.pallas_call(kernel, out_shape=(jax.ShapeDtypeStruct((units, width), f3...  76.7 us
    unnamed x8, local copies, waits for them, and re-layouts  8.53 us
    sub x1, other arithmetic, shards(): master - learn_rate * (moment_one_new / first_fix) / (jnp.sqrt(moment_two...  1.83 us

profile of v1, /device:TPU:0, one launch (start us, length us, event | category | flops | bytes accessed | tf_op | source)
XLA Modules:
  0.0 87.7 jit_solution(13840842340202419318)
XLA Ops:
  0.6 0.0 copy-start
  0.6 0.0 copy-start.1
  0.7 0.0 copy-start.2
  0.7 76.7 %gather_project_scatter.1 = (f32[48,896]{1,0:T(8,128)}, bf16[256,384]{1,0:T(8,128)(2,1)}, bf16[256,14336]{1,0:T(8,128)(2,1)}) custom-call(f32[48,896]{1,0:T(8,128)} %master.1, bf16[256,14336]{1,0:T(8,128)(2,1)} %tokens.1, bf16[256,384]{1,0:T(8,128)(2,1)} %cot.1), custom_call_target="tpu_custom_call" | custom-call | tf_op jit(solution)/shard_map/gather_project_scatter/pallas_call | solution.py:344
  77.3 0.0 copy-done
  77.3 0.0 copy-done.1
  77.4 0.0 copy-done.2
  77.4 1.8 %divide_subtract_fusion = (f32[48,896]{1,0:T(8,128)}, f32[48,896]{1,0:T(8,128)}, f32[48,896]{1,0:T(8,128)}, f32[48,896]{1,0:T(8,128)}) fusion(f32[48,896]{1,0:T(8,128)S(1)} %copy-done, f32[48,896]{1,0:T(8,128)} %get-tuple-element.11, f32[48,896]{1,0:T(8,128)S(1)} %copy-done.1, f32[48,896]{1,0:T(8,128)S(1)} %copy-done.2), kind=kLoop, calls=%fused_computation | loop fusion | flops 559104 | bytes 1376256 | tf_op jit(solution)/shard_map/sub | solution.py:383
  79.2 1.6 %copy.13 = bf16[256,384]{1,0:T(8,128)(2,1)} copy(bf16[256,384]{1,0:T(8,128)(2,1)} %get-tuple-element.22) | data formatting | bytes 393216
  80.8 6.9 %copy.14 = bf16[256,14336]{1,0:T(8,128)(2,1)} copy(bf16[256,14336]{1,0:T(8,128)(2,1)} %get-tuple-element.23) | data formatting | bytes 14680064
Async XLA Ops:
  0.6 76.7 %copy-start = (f32[48,896]{1,0:T(8,128)S(1)}, f32[48,896]{1,0:T(8,128)}, u32[]{:S(2)}) copy-start(f32[48,896]{1,0:T(8,128)} %master.1) | copy-start | bytes 516100
  0.6 76.7 %copy-start.1 = (f32[48,896]{1,0:T(8,128)S(1)}, f32[48,896]{1,0:T(8,128)}, u32[]{:S(2)}) copy-start(f32[48,896]{1,0:T(8,128)} %param.8) | copy-start | bytes 516100
  0.7 76.7 %copy-start.2 = (f32[48,896]{1,0:T(8,128)S(1)}, f32[48,896]{1,0:T(8,128)}, u32[]{:S(2)}) copy-start(f32[48,896]{1,0:T(8,128)} %param.9) | copy-start | bytes 516100

commit v2 on v0

v2 whole, which is shorter than its diff:
```python
import functools

import jax
import jax.numpy as jnp
from jax import lax
from jax.experimental import pallas as pl
from jax.experimental.pallas import tpu as pltpu
from jax.sharding import PartitionSpec as P

MESH = pl.DeviceIdType.MESH
STEP = 10

beta_one = 0.9
beta_two = 0.95
learn_rate = 0.001
adam_eps = 1e-08
gelu_coef = 0.7978845608
gelu_cube = 0.044715

ORDERS = (("x", "y", "z"), ("y", "z", "x"), ("z", "x", "y"))
ROWS = 16
GROUPS = 3
COLUMNS = ((0, 384), (384, 256), (640, 256))
WIDEST = 384
AG_DIRECT = (True, False, False)
RS_DIRECT = (False, False, True)


(
    LINE, PLANE, PLANE_ON, CUBE, CUBE_ON, TOKENS_OUT, TOKENS_IN, COT_TURN, FORWARD, PARTIAL_OUT,
    ACTIVATE, TERM, FAR, BACK, RS_CUBE_ON, RS_PLANE, RS_PLANE_ON, RS_LINE, RS_END, ACT_TURN, INPUT,
    HIDDEN,
) = range(22)
SCHEDULE = (
    (LINE, 0, 2), (LINE, 0, 0), (LINE, 0, 1), (LINE, 1, 0), (LINE, 2, 2), (TOKENS_OUT,), (LINE, 2, 0), (LINE, 2, 1),
    (LINE, 1, 1), (LINE, 1, 2), (PLANE, 0, 2), (PLANE, 0, 1), (PLANE, 0, 0), (PLANE, 1, 0), (PLANE, 1, 2),
    (PLANE, 1, 1), (PLANE, 2, 2), (PLANE, 2, 1), (CUBE, 0, 1, 0), (CUBE, 0, 2, 0), (CUBE, 0, 0, 0), (PLANE_ON, 1, 2),
    (CUBE, 0, 2, 1), (CUBE, 0, 1, 1), (CUBE, 0, 0, 1), (TOKENS_IN, 0), (FORWARD, 0, 0, 0), (PLANE, 2, 0),
    (PLANE_ON, 1, 1), (CUBE, 1, 1, 0), (CUBE_ON, 0, 1, 0), (PLANE_ON, 1, 0), (CUBE_ON, 0, 2, 0), (CUBE_ON, 0, 2, 1),
    (CUBE, 1, 2, 0), (CUBE, 1, 2, 1), (CUBE_ON, 0, 1, 1), (TOKENS_IN, 1), (CUBE_ON, 0, 0, 0), (TOKENS_IN, 2),
    (COT_TURN,), (CUBE_ON, 0, 0, 1), (CUBE, 1, 0, 0), (FORWARD, 0, 0, 1), (TOKENS_IN, 3), (CUBE, 1, 0, 1),
    (PLANE_ON, 2, 0), (CUBE_ON, 1, 1, 0), (FORWARD, 1, 0, 0), (FORWARD, 0, 2, 0), (PLANE_ON, 2, 2),
    (FORWARD, 0, 0, 2), (CUBE, 2, 2, 0), (CUBE, 1, 1, 1), (FORWARD, 0, 2, 1), (FORWARD, 0, 1, 0), (FORWARD, 0, 1, 1),
    (FORWARD, 0, 0, 3), (PARTIAL_OUT, 0), (PLANE_ON, 2, 1), (CUBE, 2, 1, 0), (CUBE, 2, 0, 0), (CUBE_ON, 1, 2, 0),
    (CUBE_ON, 1, 2, 1), (FORWARD, 1, 1, 0), (CUBE, 2, 2, 1), (FORWARD, 1, 2, 0), (CUBE_ON, 1, 1, 1),
    (CUBE_ON, 1, 0, 0), (CUBE_ON, 1, 0, 1), (FORWARD, 1, 0, 1), (CUBE, 2, 0, 1), (ACTIVATE, 0), (TERM, 0, 0),
    (FAR, 0, 0, 1), (CUBE, 2, 1, 1), (TERM, 0, 1), (TERM, 0, 2), (BACK, 0, 0, 0), (CUBE_ON, 2, 0, 0), (FAR, 0, 2, 1),
    (FAR, 0, 2, 0), (TERM, 0, 3), (BACK, 0, 2, 1), (FAR, 0, 1, 1), (FAR, 0, 1, 0), (FORWARD, 1, 0, 2),
    (FORWARD, 1, 2, 1), (FORWARD, 1, 1, 1), (BACK, 0, 1, 0), (FORWARD, 1, 0, 3), (PARTIAL_OUT, 1), (CUBE_ON, 2, 2, 0),
    (BACK, 0, 2, 0), (CUBE_ON, 2, 0, 1), (BACK, 0, 1, 1), (CUBE_ON, 2, 2, 1), (BACK, 0, 0, 1), (CUBE_ON, 2, 1, 0),
    (CUBE_ON, 2, 1, 1), (FORWARD, 2, 2, 0), (FORWARD, 2, 0, 1), (FORWARD, 2, 0, 0), (FORWARD, 2, 0, 2),
    (RS_CUBE_ON, 0, 1, 1), (RS_CUBE_ON, 0, 2, 1), (FAR, 0, 0, 0), (RS_CUBE_ON, 0, 0, 1), (RS_CUBE_ON, 0, 1, 0),
    (ACTIVATE, 1), (TERM, 1, 0), (TERM, 1, 1), (FAR, 1, 2, 1), (FAR, 1, 2, 0), (TERM, 1, 2), (TERM, 1, 3),
    (BACK, 1, 2, 0), (FAR, 1, 0, 1), (FAR, 1, 1, 1), (FAR, 1, 1, 0), (FORWARD, 2, 1, 0), (FORWARD, 2, 0, 3),
    (FORWARD, 2, 1, 1), (BACK, 1, 2, 1), (FORWARD, 2, 2, 1), (PARTIAL_OUT, 2), (FAR, 1, 0, 0), (BACK, 1, 0, 0),
    (BACK, 1, 0, 1), (BACK, 1, 1, 1), (BACK, 1, 1, 0), (RS_PLANE, 0, 2, 1), (RS_CUBE_ON, 0, 2, 0),
    (RS_PLANE, 0, 1, 1), (RS_CUBE_ON, 0, 0, 0), (RS_CUBE_ON, 1, 2, 1), (RS_CUBE_ON, 1, 2, 0), (RS_CUBE_ON, 1, 1, 1),
    (RS_PLANE, 0, 0, 1), (ACTIVATE, 2), (TERM, 2, 0), (TERM, 2, 1), (FAR, 2, 2, 1), (FAR, 2, 0, 1),
    (RS_CUBE_ON, 1, 0, 1), (RS_CUBE_ON, 1, 1, 0), (FAR, 2, 2, 0), (TERM, 2, 2), (FAR, 2, 0, 0), (TERM, 2, 3),
    (BACK, 2, 2, 0), (FAR, 2, 1, 1), (FAR, 2, 1, 0), (BACK, 2, 2, 1), (BACK, 2, 1, 0), (RS_CUBE_ON, 1, 0, 0),
    (ACT_TURN,), (INPUT, 0), (RS_PLANE, 1, 2, 1), (RS_PLANE, 1, 2, 0), (RS_PLANE, 1, 1, 1), (RS_CUBE_ON, 2, 0, 1),
    (BACK, 2, 0, 1), (BACK, 2, 0, 0), (BACK, 2, 1, 1), (RS_CUBE_ON, 2, 2, 1), (INPUT, 1), (RS_CUBE_ON, 2, 1, 1),
    (RS_CUBE_ON, 2, 2, 0), (RS_CUBE_ON, 2, 0, 0), (RS_PLANE, 0, 2, 0), (RS_PLANE, 1, 0, 1), (RS_CUBE_ON, 2, 1, 0),
    (RS_PLANE_ON, 0, 2), (RS_PLANE, 0, 0, 0), (RS_PLANE_ON, 0, 0), (RS_PLANE, 0, 1, 0), (RS_PLANE_ON, 1, 2),
    (RS_PLANE, 1, 1, 0), (RS_PLANE_ON, 1, 1), (INPUT, 2), (RS_PLANE, 2, 2, 1), (RS_PLANE, 2, 0, 1),
    (RS_PLANE, 2, 1, 1), (RS_PLANE, 1, 0, 0), (RS_PLANE, 2, 2, 0), (RS_PLANE_ON, 0, 1), (RS_PLANE_ON, 1, 0),
    (RS_PLANE, 2, 1, 0), (RS_PLANE, 2, 0, 0), (INPUT, 3), (RS_LINE, 0, 0), (RS_LINE, 1, 1), (RS_LINE, 0, 2),
    (RS_LINE, 1, 0), (RS_LINE, 1, 2), (RS_LINE, 0, 1), (RS_LINE, 2, 2), (RS_LINE, 2, 1), (RS_LINE, 2, 0),
    (RS_END, 1, 0), (RS_END, 0, 2), (HIDDEN,), (RS_END, 0, 1), (RS_END, 0, 0), (RS_END, 1, 2), (RS_END, 1, 1),
    (RS_END, 2, 1), (RS_END, 2, 2), (RS_END, 2, 0),
)


def wrap(value):
    return lax.rem(value + 4, 4)


def device(at, core):
    node = at["z"] * 4 + (at["y"] // 2) * 2 + core
    local = lax.rem(at["y"], 2) * 4 + at["x"]
    return (node, local)


def kernel(
    master_hbm, tokens, cot_hbm, out_grad, out_hidden, out_input,
    weights, tok, terms, acc, pre_in, act_t, act, cot_t, hid_t, stage, master, cot,
    hop_a0, hop_a1, hop_a2, hop_b0, hop_b1, hop_b2, hop_c0, hop_c1, hop_c2, row_a, row_b, row_c, last_in,
    own_sem, tok_sem, tok_send, tok_recv, pre_send, pre_recv, cot_send, cot_recv, in_send, in_recv,
    ag_send, ag_recv, rs_send, rs_recv,
):
    hop_a, hop_b, hop_c = (hop_a0, hop_a1, hop_a2), (hop_b0, hop_b1, hop_b2), (hop_c0, hop_c1, hop_c2)
    node, local = lax.axis_index("node"), lax.axis_index("local")
    core = lax.rem(node, 2)
    me = {"x": lax.rem(local, 4), "y": lax.rem(node // 2, 2) * 2 + local // 4, "z": node // 4}
    sign = 1 - 2 * core
    own = [
        pltpu.make_async_copy(master_hbm, master, own_sem.at[0]),
        pltpu.make_async_copy(cot_hbm, cot.at[core], own_sem.at[1]),
    ]
    for copy in own:
        copy.start()
    width = master.shape[1]
    half = tokens.shape[0]
    units = 8 * ROWS
    groups, orders = range(GROUPS), range(len(ORDERS))

    def near(dim, step):
        at = dict(me)
        at[dim] = wrap(at[dim] + step)
        return device(at, core)

    partner = device(me, 1 - core)
    around = [near(dim, step) for dim in "xyz" for step in (1, 3, 2)] + [partner]
    barrier = pltpu.get_barrier_semaphore()
    for other in around:
        pl.semaphore_signal(barrier, inc=1, device_id=other, device_id_type=MESH)

    mine = pl.ds(pl.multiple_of(core * half, half), half)
    theirs = pl.ds(pl.multiple_of((1 - core) * half, half), half)

    def columns_of(k, which):
        return pl.ds(pl.multiple_of((2 * k + which) * width, 128), width)

    def chunk(i):
        z = wrap(me["z"] + (0, -sign, sign, 2)[i // 2])
        return 2 * z + i % 2

    def own_tokens(i):
        k = chunk(i)
        return pltpu.make_async_copy(tokens.at[:, columns_of(k, core)], tok.at[k, mine, :], tok_sem.at[k])

    for i in range(8):
        own_tokens(i).start()
    own[0].wait()
    weights[me["z"], me["y"], me["x"]] = master[...].astype(jnp.bfloat16)
    acc[...] = jnp.zeros_like(acc)
    pl.semaphore_wait(barrier, len(around))

    sent = []

    def send(src, dst, send_sem, recv_sem, to):
        copy = pltpu.make_async_remote_copy(
            src_ref=src, dst_ref=dst, send_sem=send_sem, recv_sem=recv_sem, device_id=to, device_id_type=MESH
        )
        copy.start()
        sent.append(copy)

    def arrived(dst, send_sem, recv_sem):
        pltpu.make_async_remote_copy(
            src_ref=dst, dst_ref=dst, send_sem=send_sem, recv_sem=recv_sem, device_id=partner, device_id_type=MESH
        ).wait_recv()

    def columns(g, o):
        return COLUMNS[(o - g) % len(COLUMNS)]

    def block(buf, g, o, place):
        first, count = columns(g, o)
        return buf.at[tuple(place[d] for d in "zyx") + (pl.ds(g * ROWS, ROWS), pl.ds(first, count))]

    def cut(buf, g, o):
        return buf.at[..., pl.ds(0, columns(g, o)[1])]

    line = pl.ds(0, 4)

    def pair(dim, far):
        upper = me[dim] // 2
        return pl.ds(2 * (1 - upper if far else upper), 2)

    def ag(g, o, msg, place, to):
        region = block(weights, g, o, place)
        send(region, region, ag_send.at[3 * g + o, msg], ag_recv.at[3 * g + o, msg], to)

    def ag_wait(g, o, msg, place):
        arrived(block(weights, g, o, place), ag_send.at[3 * g + o, msg], ag_recv.at[3 * g + o, msg])

    def row(o, step):
        one, two, three = ORDERS[o]
        return {one: line, two: wrap(me[two] + step), three: me[three]}

    def rows(o, far, step):
        one, two, three = ORDERS[o]
        return {one: line, two: pair(two, far), three: wrap(me[three] + step)}

    def ag_line(g, o):
        for i, step in enumerate((1, 3, 2)):
            ag(g, o, i, me, near(ORDERS[o][0], step))

    def ag_plane(g, o):
        one, two, three = ORDERS[o]
        for i, step in enumerate((1, 3, 2)):
            ag_wait(g, o, i, {**me, one: wrap(me[one] - step)})
        ag(g, o, 3, row(o, 0), near(two, sign))
        ag(g, o, 4, row(o, 0), near(two, -sign))
        if AG_DIRECT[g]:
            ag(g, o, 5, row(o, 0), near(two, 2))

    def ag_plane_on(g, o):
        ag_wait(g, o, 3, row(o, -sign))
        ag(g, o, 5, row(o, -sign), near(ORDERS[o][1], sign))

    def ag_cube(g, o, far):
        three = ORDERS[o][2]
        if AG_DIRECT[g] and not far:
            ag_wait(g, o, 3, row(o, -sign))
        ag_wait(g, o, 4 + far, row(o, 2 if far else sign))
        ag(g, o, 6 + 3 * far, rows(o, far, 0), near(three, sign))
        ag(g, o, 7 + 3 * far, rows(o, far, 0), near(three, -sign))

    def ag_cube_on(g, o, far):
        ag_wait(g, o, 6 + 3 * far, rows(o, far, -sign))
        ag(g, o, 8 + 3 * far, rows(o, far, -sign), near(ORDERS[o][2], sign))

    def from_front(g, o, far):
        ag_wait(g, o, 7 + 3 * far, rows(o, far, sign))

    def from_across(g, o, far):
        ag_wait(g, o, 8 + 3 * far, rows(o, far, 2))

    def tokens_out():
        send(cot_hbm, cot.at[core], cot_send, cot_recv, partner)
        for i in range(8):
            k = chunk(i)
            send(tokens.at[:, columns_of(k, 1 - core)], tok.at[k, mine, :], tok_send.at[k], tok_recv.at[k], partner)

    def tokens_in(i):
        for j in (2 * i, 2 * i + 1):
            own_tokens(j).wait()
            k = chunk(j)
            arrived(tok.at[k, theirs, :], tok_send.at[k], tok_recv.at[k])

    def cot_turn():
        own[1].wait()
        arrived(cot.at[1 - core], cot_send, cot_recv)
        turned = cot[...].reshape(2 * half, GROUPS * units).astype(jnp.float32).T
        cot_t[...] = turned.astype(jnp.bfloat16).reshape(8, GROUPS, ROWS, 2 * half)

    def forward(g, o, i):
        if (o, i) in ((0, 2), (2, 0)):
            from_front(g, o, 0)
            from_front(g, o, 1)
        if (o, i) in ((0, 3), (2, 1)):
            from_across(g, o, 0)
            from_across(g, o, 1)
        if o == 1:
            from_front(g, o, i)
            from_across(g, o, i)
        first, count = columns(g, o)
        here = pl.ds(first, count)

        total = acc[g]
        for j in range(2 if o == 0 else 4):
            z, upper = j // 2, j % 2
            if o == 0:
                z = wrap(me["z"] + (0, -sign, sign, 2)[i])
            elif o == 1:
                z = lax.rem(me["z"] // 2 + i, 2) * 2 + z
            else:
                z, upper = j, lax.rem(me["y"] // 2 + i, 2)
            part = weights[z, pl.ds(2 * upper, 2), :, pl.ds(g * ROWS, ROWS), here].reshape(units, count)
            total += lax.dot_general(
                part, tok[2 * z + upper, :, here], (((1,), (1,)), ((), ())), preferred_element_type=jnp.float32
            )
        acc[g] = total

    def partial_out(g):
        send(acc.at[g], pre_in.at[g], pre_send.at[g], pre_recv.at[g], partner)

    def activate(g):
        arrived(pre_in.at[g], pre_send.at[g], pre_recv.at[g])
        pre = acc[g] + pre_in[g]
        tanh_val = jnp.tanh(gelu_coef * (pre + gelu_cube * pre * pre * pre))
        inner = gelu_coef * (1.0 + 3.0 * gelu_cube * pre * pre)
        slope = 0.5 * (1.0 + tanh_val) + 0.5 * pre * (1.0 - tanh_val * tanh_val) * inner
        slope *= cot_t[:, g].reshape(units, 2 * half).astype(jnp.float32)
        act_t[:, g] = slope.astype(jnp.bfloat16).reshape(8, ROWS, 2 * half)
        hid_t[:, g] = (0.5 * pre * (1.0 + tanh_val)).reshape(8, ROWS, 2 * half)

    def rs(g, o, msg, src, dst, to):
        send(src, dst, rs_send.at[3 * g + o, msg], rs_recv.at[3 * g + o, msg], to)

    def rs_wait(g, o, msg, dst):
        arrived(dst, rs_send.at[3 * g + o, msg], rs_recv.at[3 * g + o, msg])

    def add(dst, *values):
        total = values[0][...].astype(jnp.float32)
        for value in values[1:]:
            total += value[...].astype(jnp.float32)
        dst[...] = total.astype(dst.dtype)

    def term(g, i):
        upper = lax.rem(me["y"] // 2 + (1 if i < 2 else 0), 2)

        for step in (2, -sign) if i % 2 == 0 else (sign, 0):
            z = wrap(me["z"] + step)
            value = jnp.dot(act_t[:, g].reshape(units, 2 * half), tok[2 * z + upper], preferred_element_type=jnp.float32)
            terms[z, pl.ds(2 * upper, 2), :, pl.ds(g * ROWS, ROWS), :] = value.astype(jnp.bfloat16).reshape(
                2, 4, ROWS, width
            )

    def rs_far(g, o, far):
        hop = cut(hop_a[o].at[g, far], g, o)
        rs(g, o, 3 * far, block(terms, g, o, rows(o, far, 2)), hop, near(ORDERS[o][2], sign))

    def rs_back(g, o, far):
        hop = cut(hop_c[o].at[g, far], g, o)
        rs(g, o, 3 * far + 2, block(terms, g, o, rows(o, far, -sign)), hop, near(ORDERS[o][2], -sign))

    def add_pair(g, o, far, into_hop, plane, *hops):
        one, two, three = ORDERS[o]
        upper = me[two] // 2
        first = 2 * (1 - upper if far else upper)

        def step(i, carry):
            here = block(terms, g, o, {one: line, two: first + i, three: wrap(me[three] + plane)})
            views = [cut(hop.at[g, far, :, i] if o == 2 else hop.at[g, far, i], g, o) for hop in hops]
            add(views[0] if into_hop else here, here, *views)
            return carry

        lax.fori_loop(0, 2, step, 0)

    def rs_cube_on(g, o, far):
        hop = cut(hop_a[o].at[g, far], g, o)
        rs_wait(g, o, 3 * far, hop)
        add_pair(g, o, far, True, sign, hop_a[o])
        rs(g, o, 3 * far + 1, hop, cut(hop_b[o].at[g, far], g, o), near(ORDERS[o][2], sign))

    def rs_plane(g, o, far):
        rs_wait(g, o, 3 * far + 1, cut(hop_b[o].at[g, far], g, o))
        rs_wait(g, o, 3 * far + 2, cut(hop_c[o].at[g, far], g, o))
        add_pair(g, o, far, False, 0, hop_b[o], hop_c[o])
        two = ORDERS[o][1]
        if far:
            rs(g, o, 6, block(terms, g, o, row(o, 2)), cut(row_a.at[g, o], g, o), near(two, 2 if RS_DIRECT[g] else sign))
        else:
            rs(g, o, 8, block(terms, g, o, row(o, -sign)), cut(row_c.at[g, o], g, o), near(two, -sign))
            if RS_DIRECT[g]:
                rs(g, o, 7, block(terms, g, o, row(o, sign)), cut(row_b.at[g, o], g, o), near(two, sign))

    def rs_plane_on(g, o):
        here = cut(row_a.at[g, o], g, o)
        rs_wait(g, o, 6, here)
        add(here, here, block(terms, g, o, row(o, sign)))
        rs(g, o, 7, here, cut(row_b.at[g, o], g, o), near(ORDERS[o][1], sign))

    def rs_line(g, o):
        from_back, from_ahead = cut(row_b.at[g, o], g, o), cut(row_c.at[g, o], g, o)
        rs_wait(g, o, 7, from_back)
        rs_wait(g, o, 8, from_ahead)
        here = block(terms, g, o, row(o, 0))
        if RS_DIRECT[g]:
            across = cut(row_a.at[g, o], g, o)
            rs_wait(g, o, 6, across)
            add(here, here, from_back, from_ahead, across)
        else:
            add(here, here, from_back, from_ahead)
        one = ORDERS[o][0]
        for i, step in enumerate((2, 1, 3)):
            rs(
                g, o, 9 + i, block(terms, g, o, {**me, one: wrap(me[one] + step)}),
                cut(last_in.at[g, o, i], g, o), near(one, step),
            )

    def rs_end(g, o):
        views = [cut(last_in.at[g, o, i], g, o) for i in range(3)]
        for i, view in enumerate(views):
            rs_wait(g, o, 9 + i, view)
        first, count = columns(g, o)
        add(out_grad.at[pl.ds(g * ROWS, ROWS), pl.ds(first, count)], block(terms, g, o, me), *views)

    def act_turn():
        act[...] = act_t[...].reshape(GROUPS * units, 2 * half).astype(jnp.float32).T.astype(jnp.bfloat16)

    def hidden_turn():
        out_hidden[...] = hid_t[:, :, :, mine].reshape(GROUPS * units, half).T.astype(jnp.bfloat16)

    def input_chunks(i):
        for k in (2 * i, 2 * i + 1):
            weight = weights[k // 2, pl.ds(2 * (k % 2), 2)].reshape(GROUPS * units, width)
            here = columns_of(k, core)
            stage[k] = jnp.dot(act[theirs, :], weight, preferred_element_type=jnp.float32).astype(jnp.bfloat16)
            send(stage.at[k], out_input.at[:, here], in_send.at[k], in_recv.at[k], partner)
            out_input[:, here] = jnp.dot(act[mine, :], weight, preferred_element_type=jnp.float32).astype(jnp.bfloat16)

    steps = (
        ag_line, ag_plane, ag_plane_on, ag_cube, ag_cube_on, tokens_out, tokens_in, cot_turn, forward, partial_out,
        activate, term, rs_far, rs_back, rs_cube_on, rs_plane, rs_plane_on, rs_line, rs_end, act_turn, input_chunks,
        hidden_turn,
    )
    for name, *where in SCHEDULE:
        steps[name](*where)
    for k in range(8):
        arrived(out_input.at[:, columns_of(k, 1 - core)], in_send.at[k], in_recv.at[k])
    for copy in sent:
        copy.wait_send()


def update(
    blocks, total, hidden, input_grad, master, moment_one, moment_two,
    out_hidden, out_input, out_grad, out_master, out_one, out_two, old, new, in_sem, out_sem,
):
    loads = [
        pltpu.make_async_copy(value, old.at[i], in_sem.at[i]) for i, value in enumerate((moment_one, moment_two, master))
    ]
    for copy in loads:
        copy.start()
    rows = input_grad.shape[0] // 4
    copies = [
        pltpu.make_async_copy(
            input_grad.at[pl.ds(i * rows, rows)], out_input.at[pl.ds(i * rows, rows)], out_sem.at[i]
        )
        for i in range(4)
    ]
    copies.append(pltpu.make_async_copy(hidden, out_hidden, out_sem.at[4]))
    for copy in copies:
        copy.start()

    def store(i, value, out):
        new[i] = value
        copies.append(pltpu.make_async_copy(new.at[i], out, out_sem.at[5 + i]))
        copies[-1].start()

    gradient = total[...] / blocks
    store(0, gradient, out_grad)
    loads[0].wait()
    moment_one_new = beta_one * old[0] + (1.0 - beta_one) * gradient
    store(1, moment_one_new, out_one)
    loads[1].wait()
    moment_two_new = beta_two * old[1] + (1.0 - beta_two) * gradient * gradient
    store(2, moment_two_new, out_two)
    loads[2].wait()
    first_fix = 1.0 - beta_one**STEP
    second_fix = 1.0 - beta_two**STEP
    step = learn_rate * (moment_one_new / first_fix) / (jnp.sqrt(moment_two_new / second_fix) + adam_eps)
    store(3, old[2] - step, out_master)
    for copy in copies:
        copy.wait()


def shards(tokens, cotangent, master, moment_one, moment_two):
    half, model = tokens.shape
    units, width = master.shape
    all_units = cotangent.shape[1]
    bf, f32 = jnp.bfloat16, jnp.float32
    dma = pltpu.SemaphoreType.DMA
    vmem, anywhere = pl.BlockSpec(memory_space=pltpu.VMEM), pl.BlockSpec(memory_space=pl.ANY)
    total, hidden, input_grad = pl.pallas_call(
        kernel,
        out_shape=(
            pltpu.VMEM((units, width), f32),
            pltpu.VMEM((half, all_units), bf),
            pltpu.VMEM((half, model), bf),
        ),
        in_specs=[anywhere] * 3,
        out_specs=(vmem, vmem, vmem),
        scratch_shapes=[
            pltpu.VMEM((4, 4, 4, units, width), bf),
            pltpu.VMEM((8, 2 * half, width), bf),
            pltpu.VMEM((4, 4, 4, units, width), bf),
            pltpu.VMEM((GROUPS, 8 * ROWS, 2 * half), f32),
            pltpu.VMEM((GROUPS, 8 * ROWS, 2 * half), f32),
            pltpu.VMEM((8, GROUPS, ROWS, 2 * half), bf),
            pltpu.VMEM((2 * half, all_units), bf),
            pltpu.VMEM((8, GROUPS, ROWS, 2 * half), bf),
            pltpu.VMEM((8, GROUPS, ROWS, 2 * half), f32),
            pltpu.VMEM((8, half, width), bf),
            pltpu.VMEM((units, width), f32),
            pltpu.VMEM((2, half, all_units), bf),
            *(pltpu.VMEM((GROUPS, 2) + ((4, 2) if o == 2 else (2, 4)) + (ROWS, WIDEST), bf) for _ in "abc" for o in range(3)),
            pltpu.VMEM((GROUPS, 3, 4, ROWS, WIDEST), bf),
            pltpu.VMEM((GROUPS, 3, 4, ROWS, WIDEST), bf),
            pltpu.VMEM((GROUPS, 3, 4, ROWS, WIDEST), bf),
            pltpu.VMEM((GROUPS, 3, 3, ROWS, WIDEST), bf),
            dma((2,)), dma((8,)), dma((8,)), dma((8,)), dma((GROUPS,)), dma((GROUPS,)), dma, dma,
            dma((8,)), dma((8,)),
            dma((3 * GROUPS, 12)), dma((3 * GROUPS, 12)), dma((3 * GROUPS, 12)), dma((3 * GROUPS, 12)),
        ],
        compiler_params=pltpu.CompilerParams(
            collective_id=0, has_side_effects=True, vmem_limit_bytes=40 * 2**20
        ),
        name="gather_project_scatter",
    )(*(pltpu.with_memory_space_constraint(value, pltpu.HBM) for value in (master, tokens, cotangent)))
    state = jax.ShapeDtypeStruct((units, width), f32)
    in_vmem = (pltpu.with_memory_space_constraint(value, pltpu.VMEM) for value in (total, hidden, input_grad))
    return pl.pallas_call(
        functools.partial(update, lax.axis_size("node") * lax.axis_size("local")),
        out_shape=(
            jax.ShapeDtypeStruct((half, all_units), bf),
            jax.ShapeDtypeStruct((half, model), bf),
            state, state, state, state,
        ),
        in_specs=[vmem] * 3 + [anywhere] * 3,
        out_specs=(anywhere,) * 6,
        scratch_shapes=[pltpu.VMEM((3, units, width), f32), pltpu.VMEM((4, units, width), f32), dma((3,)), dma((9,))],
        compiler_params=pltpu.CompilerParams(vmem_limit_bytes=16 * 2**20),
        name="adam_and_store",
    )(*in_vmem, *(pltpu.with_memory_space_constraint(value, pltpu.HBM) for value in (master, moment_one, moment_two)))


def solution(mesh):
    in_specs = (
        P(("node", "local"), None),
        P(("node", "local"), None),
        P("local", "node"),
        P("local", "node"),
        P("local", "node"),
    )
    out_specs = (
        P(("node", "local"), None),
        P(("node", "local"), None),
        P("local", "node"),
        P("local", "node"),
        P("local", "node"),
        P("local", "node"),
    )
    return jax.shard_map(shards, mesh=mesh, in_specs=in_specs, out_specs=out_specs, check_vma=False)
```

time: 401 us -> 71.4 us (0.18)
  waiting for transfers between devices: 348 us -> 0 us
  Pallas kernels: 0 us -> 70.4 us
  matrix products: 29.3 us -> 0 us
  between operations: 13.8 us -> 0.8 us
  local copies, waits for them, and re-layouts: 7.39 us -> 0 us
    all_gather x2 -> x0, waiting for transfers between devices: 166 us -> none  [the longest x1 116 us: shards(): lax.all_gather(secondary, 'local', axis=0, tiled=True)]
    reduce_scatter x1 -> x0, waiting for transfers between devices: 116 us -> none  [shards(): lax.psum_scatter(product.astype(jnp.bfloat16).astype(jnp.float32).astype(...]
    pallas_call x0 -> x2, Pallas kernels: none -> 70.4 us  [the longest x1 67.1 us: shards(): pl.pallas_call(kernel, out_shape=(pltpu.VMEM((units, width), f32), pltpu....]
    unnamed x5 -> x0, waiting for transfers between devices: 65.4 us -> none
    dot_general x3 -> x0, matrix products: 29.3 us -> none  [the longest x1 10.5 us: units_to_width(): lax.dot_general(unit_grad, weight_rows, (((0,), (0,)), ((), ())), preferr...]
    unnamed x10 -> x0, local copies, waits for them, and re-layouts: 7.39 us -> none
  transfers between devices with their start and end apart: 4 -> 0, of which waited for: 4 -> 0; matrix products, arithmetic and copies ran while one was open for 3% -> 0% of each run, Pallas kernels for 0% -> 0%
where the time goes in v2:
time: 71.4 us; the launch traced here: 71.2 us
  Pallas kernels  70.4 us (99%)
  between operations  0.8 us (1%)
    pallas_call x1, Pallas kernels, shards(): pl.pallas_call(kernel, out_shape=(pltpu.VMEM((units, width), f32), pltpu....  67.1 us
    pallas_call x1, Pallas kernels, shards(): pl.pallas_call(functools.partial(update, lax.axis_size('node') * lax.axis...  3.36 us

profile of v2, /device:TPU:0, one launch (start us, length us, event | category | flops | bytes accessed | tf_op | source)
XLA Modules:
  0.0 71.2 jit_solution(7094040832711659759)
XLA Ops:
  0.6 67.1 %gather_project_scatter.1 = (f32[48,896]{1,0:T(8,128)S(1)}, bf16[256,384]{1,0:T(8,128)(2,1)S(1)}, bf16[256,14336]{1,0:T(8,128)(2,1)S(1)}) custom-call(f32[48,896]{1,0:T(8,128)} %master.1, bf16[256,14336]{1,0:T(8,128)(2,1)} %tokens.1, bf16[256,384]{1,0:T(8,128)(2,1)} %cot_hbm.1), custom_call_target="tpu_custom_call" | custom-call | tf_op jit(solution)/shard_map/gather_project_scatter/pallas_call | solution.py:446
  67.7 3.4 %adam_and_store.1 = (bf16[256,384]{1,0:T(8,128)(2,1)}, bf16[256,14336]{1,0:T(8,128)(2,1)}, f32[48,896]{1,0:T(8,128)}, f32[48,896]{1,0:T(8,128)}, f32[48,896]{1,0:T(8,128)}, /*index=5*/f32[48,896]{1,0:T(8,128)}) custom-call(f32[48,896]{1,0:T(8,128)S(1)} %get-tuple-element.9.total, bf16[256,384]{1,0:T(8,128)(2,1)S(1)} %get-tuple-element.10.hidden, ...), custom_call_target="tpu_custom_call" | custom-call | tf_op jit(solution)/shard_map/adam_and_store/pallas_call | solution.py:484

commit v3 on v2

--- a/solution.py
+++ b/solution.py
@@ -32,42 +32,42 @@
     HIDDEN,
 ) = range(22)
 SCHEDULE = (
-    (LINE, 0, 2), (LINE, 0, 0), (LINE, 0, 1), (LINE, 1, 0), (LINE, 2, 2), (TOKENS_OUT,), (LINE, 2, 0), (LINE, 2, 1),
-    (LINE, 1, 1), (LINE, 1, 2), (PLANE, 0, 2), (PLANE, 0, 1), (PLANE, 0, 0), (PLANE, 1, 0), (PLANE, 1, 2),
-    (PLANE, 1, 1), (PLANE, 2, 2), (PLANE, 2, 1), (CUBE, 0, 1, 0), (CUBE, 0, 2, 0), (CUBE, 0, 0, 0), (PLANE_ON, 1, 2),
-    (CUBE, 0, 2, 1), (CUBE, 0, 1, 1), (CUBE, 0, 0, 1), (TOKENS_IN, 0), (FORWARD, 0, 0, 0), (PLANE, 2, 0),
-    (PLANE_ON, 1, 1), (CUBE, 1, 1, 0), (CUBE_ON, 0, 1, 0), (PLANE_ON, 1, 0), (CUBE_ON, 0, 2, 0), (CUBE_ON, 0, 2, 1),
-    (CUBE, 1, 2, 0), (CUBE, 1, 2, 1), (CUBE_ON, 0, 1, 1), (TOKENS_IN, 1), (CUBE_ON, 0, 0, 0), (TOKENS_IN, 2),
-    (COT_TURN,), (CUBE_ON, 0, 0, 1), (CUBE, 1, 0, 0), (FORWARD, 0, 0, 1), (TOKENS_IN, 3), (CUBE, 1, 0, 1),
-    (PLANE_ON, 2, 0), (CUBE_ON, 1, 1, 0), (FORWARD, 1, 0, 0), (FORWARD, 0, 2, 0), (PLANE_ON, 2, 2),
-    (FORWARD, 0, 0, 2), (CUBE, 2, 2, 0), (CUBE, 1, 1, 1), (FORWARD, 0, 2, 1), (FORWARD, 0, 1, 0), (FORWARD, 0, 1, 1),
+    (LINE, 0, 2), (LINE, 0, 0), (LINE, 0, 1), (LINE, 1, 1), (LINE, 2, 2), (LINE, 2, 1), (TOKENS_OUT,), (LINE, 2, 0),
+    (LINE, 1, 2), (LINE, 1, 0), (COT_TURN,), (PLANE, 0, 2), (PLANE, 0, 1), (PLANE, 0, 0), (PLANE, 2, 1),
+    (PLANE, 1, 1), (PLANE, 1, 2), (PLANE, 1, 0), (PLANE, 2, 2), (CUBE, 0, 2, 0), (CUBE, 0, 1, 0), (CUBE, 0, 0, 0),
+    (PLANE_ON, 1, 2), (CUBE, 0, 2, 1), (TOKENS_IN, 0), (TOKENS_IN, 1), (CUBE, 0, 1, 1), (PLANE, 2, 0),
+    (CUBE, 0, 0, 1), (PLANE_ON, 1, 1), (CUBE, 1, 1, 0), (PLANE_ON, 1, 0), (CUBE_ON, 0, 2, 0), (FORWARD, 0, 0, 0),
+    (CUBE_ON, 0, 2, 1), (CUBE_ON, 0, 1, 0), (CUBE, 1, 2, 0), (CUBE, 1, 2, 1), (TOKENS_IN, 2), (CUBE_ON, 0, 0, 0),
+    (CUBE_ON, 0, 1, 1), (CUBE_ON, 0, 0, 1), (FORWARD, 0, 0, 1), (CUBE, 1, 0, 0), (CUBE, 1, 0, 1), (TOKENS_IN, 3),
+    (PLANE_ON, 2, 0), (CUBE_ON, 1, 1, 0), (FORWARD, 0, 2, 0), (FORWARD, 0, 0, 2), (PLANE_ON, 2, 2), (CUBE, 2, 2, 0),
+    (FORWARD, 1, 0, 0), (CUBE, 1, 1, 1), (FORWARD, 0, 2, 1), (FORWARD, 0, 1, 0), (FORWARD, 0, 1, 1),
     (FORWARD, 0, 0, 3), (PARTIAL_OUT, 0), (PLANE_ON, 2, 1), (CUBE, 2, 1, 0), (CUBE, 2, 0, 0), (CUBE_ON, 1, 2, 0),
-    (CUBE_ON, 1, 2, 1), (FORWARD, 1, 1, 0), (CUBE, 2, 2, 1), (FORWARD, 1, 2, 0), (CUBE_ON, 1, 1, 1),
-    (CUBE_ON, 1, 0, 0), (CUBE_ON, 1, 0, 1), (FORWARD, 1, 0, 1), (CUBE, 2, 0, 1), (ACTIVATE, 0), (TERM, 0, 0),
-    (FAR, 0, 0, 1), (CUBE, 2, 1, 1), (TERM, 0, 1), (TERM, 0, 2), (BACK, 0, 0, 0), (CUBE_ON, 2, 0, 0), (FAR, 0, 2, 1),
-    (FAR, 0, 2, 0), (TERM, 0, 3), (BACK, 0, 2, 1), (FAR, 0, 1, 1), (FAR, 0, 1, 0), (FORWARD, 1, 0, 2),
-    (FORWARD, 1, 2, 1), (FORWARD, 1, 1, 1), (BACK, 0, 1, 0), (FORWARD, 1, 0, 3), (PARTIAL_OUT, 1), (CUBE_ON, 2, 2, 0),
-    (BACK, 0, 2, 0), (CUBE_ON, 2, 0, 1), (BACK, 0, 1, 1), (CUBE_ON, 2, 2, 1), (BACK, 0, 0, 1), (CUBE_ON, 2, 1, 0),
-    (CUBE_ON, 2, 1, 1), (FORWARD, 2, 2, 0), (FORWARD, 2, 0, 1), (FORWARD, 2, 0, 0), (FORWARD, 2, 0, 2),
-    (RS_CUBE_ON, 0, 1, 1), (RS_CUBE_ON, 0, 2, 1), (FAR, 0, 0, 0), (RS_CUBE_ON, 0, 0, 1), (RS_CUBE_ON, 0, 1, 0),
-    (ACTIVATE, 1), (TERM, 1, 0), (TERM, 1, 1), (FAR, 1, 2, 1), (FAR, 1, 2, 0), (TERM, 1, 2), (TERM, 1, 3),
-    (BACK, 1, 2, 0), (FAR, 1, 0, 1), (FAR, 1, 1, 1), (FAR, 1, 1, 0), (FORWARD, 2, 1, 0), (FORWARD, 2, 0, 3),
-    (FORWARD, 2, 1, 1), (BACK, 1, 2, 1), (FORWARD, 2, 2, 1), (PARTIAL_OUT, 2), (FAR, 1, 0, 0), (BACK, 1, 0, 0),
-    (BACK, 1, 0, 1), (BACK, 1, 1, 1), (BACK, 1, 1, 0), (RS_PLANE, 0, 2, 1), (RS_CUBE_ON, 0, 2, 0),
-    (RS_PLANE, 0, 1, 1), (RS_CUBE_ON, 0, 0, 0), (RS_CUBE_ON, 1, 2, 1), (RS_CUBE_ON, 1, 2, 0), (RS_CUBE_ON, 1, 1, 1),
-    (RS_PLANE, 0, 0, 1), (ACTIVATE, 2), (TERM, 2, 0), (TERM, 2, 1), (FAR, 2, 2, 1), (FAR, 2, 0, 1),
-    (RS_CUBE_ON, 1, 0, 1), (RS_CUBE_ON, 1, 1, 0), (FAR, 2, 2, 0), (TERM, 2, 2), (FAR, 2, 0, 0), (TERM, 2, 3),
-    (BACK, 2, 2, 0), (FAR, 2, 1, 1), (FAR, 2, 1, 0), (BACK, 2, 2, 1), (BACK, 2, 1, 0), (RS_CUBE_ON, 1, 0, 0),
-    (ACT_TURN,), (INPUT, 0), (RS_PLANE, 1, 2, 1), (RS_PLANE, 1, 2, 0), (RS_PLANE, 1, 1, 1), (RS_CUBE_ON, 2, 0, 1),
-    (BACK, 2, 0, 1), (BACK, 2, 0, 0), (BACK, 2, 1, 1), (RS_CUBE_ON, 2, 2, 1), (INPUT, 1), (RS_CUBE_ON, 2, 1, 1),
-    (RS_CUBE_ON, 2, 2, 0), (RS_CUBE_ON, 2, 0, 0), (RS_PLANE, 0, 2, 0), (RS_PLANE, 1, 0, 1), (RS_CUBE_ON, 2, 1, 0),
-    (RS_PLANE_ON, 0, 2), (RS_PLANE, 0, 0, 0), (RS_PLANE_ON, 0, 0), (RS_PLANE, 0, 1, 0), (RS_PLANE_ON, 1, 2),
-    (RS_PLANE, 1, 1, 0), (RS_PLANE_ON, 1, 1), (INPUT, 2), (RS_PLANE, 2, 2, 1), (RS_PLANE, 2, 0, 1),
-    (RS_PLANE, 2, 1, 1), (RS_PLANE, 1, 0, 0), (RS_PLANE, 2, 2, 0), (RS_PLANE_ON, 0, 1), (RS_PLANE_ON, 1, 0),
-    (RS_PLANE, 2, 1, 0), (RS_PLANE, 2, 0, 0), (INPUT, 3), (RS_LINE, 0, 0), (RS_LINE, 1, 1), (RS_LINE, 0, 2),
-    (RS_LINE, 1, 0), (RS_LINE, 1, 2), (RS_LINE, 0, 1), (RS_LINE, 2, 2), (RS_LINE, 2, 1), (RS_LINE, 2, 0),
-    (RS_END, 1, 0), (RS_END, 0, 2), (HIDDEN,), (RS_END, 0, 1), (RS_END, 0, 0), (RS_END, 1, 2), (RS_END, 1, 1),
-    (RS_END, 2, 1), (RS_END, 2, 2), (RS_END, 2, 0),
+    (CUBE_ON, 1, 2, 1), (CUBE_ON, 1, 0, 0), (FORWARD, 1, 1, 0), (CUBE, 2, 2, 1), (FORWARD, 1, 2, 0),
+    (CUBE_ON, 1, 1, 1), (CUBE_ON, 1, 0, 1), (FORWARD, 1, 0, 1), (CUBE, 2, 0, 1), (ACTIVATE, 0), (TERM, 0, 0),
+    (CUBE, 2, 1, 1), (TERM, 0, 1), (FAR, 0, 2, 1), (FAR, 0, 2, 0), (TERM, 0, 2), (TERM, 0, 3), (FAR, 0, 0, 1),
+    (FAR, 0, 0, 0), (FAR, 0, 1, 1), (FAR, 0, 1, 0), (BACK, 0, 2, 0), (BACK, 0, 2, 1), (BACK, 0, 1, 0),
+    (FORWARD, 1, 0, 2), (FORWARD, 1, 2, 1), (FORWARD, 1, 1, 1), (FORWARD, 1, 0, 3), (PARTIAL_OUT, 1),
+    (CUBE_ON, 2, 1, 0), (CUBE_ON, 2, 1, 1), (CUBE_ON, 2, 0, 0), (CUBE_ON, 2, 0, 1), (BACK, 0, 1, 1), (BACK, 0, 0, 0),
+    (CUBE_ON, 2, 2, 0), (CUBE_ON, 2, 2, 1), (FORWARD, 2, 2, 0), (FORWARD, 2, 0, 0), (FORWARD, 2, 0, 2),
+    (BACK, 0, 0, 1), (RS_CUBE_ON, 0, 2, 1), (RS_CUBE_ON, 0, 1, 1), (FORWARD, 2, 0, 1), (RS_CUBE_ON, 0, 0, 1),
+    (RS_CUBE_ON, 0, 1, 0), (ACTIVATE, 1), (TERM, 1, 0), (TERM, 1, 1), (TERM, 1, 2), (FAR, 1, 0, 1), (FAR, 1, 2, 1),
+    (TERM, 1, 3), (FAR, 1, 2, 0), (BACK, 1, 2, 1), (BACK, 1, 2, 0), (FAR, 1, 1, 1), (FORWARD, 2, 1, 0),
+    (FORWARD, 2, 1, 1), (FAR, 1, 1, 0), (FORWARD, 2, 0, 3), (FORWARD, 2, 2, 1), (PARTIAL_OUT, 2), (BACK, 1, 1, 1),
+    (FAR, 1, 0, 0), (BACK, 1, 1, 0), (BACK, 1, 0, 0), (RS_CUBE_ON, 0, 2, 0), (RS_PLANE, 0, 1, 1),
+    (RS_CUBE_ON, 1, 2, 1), (RS_CUBE_ON, 1, 2, 0), (RS_CUBE_ON, 1, 1, 1), (RS_CUBE_ON, 0, 0, 0), (RS_PLANE, 0, 0, 1),
+    (RS_PLANE, 0, 2, 1), (BACK, 1, 0, 1), (ACTIVATE, 2), (TERM, 2, 0), (TERM, 2, 1), (ACT_TURN, 1), (INPUT, 0, 1),
+    (FAR, 2, 2, 1), (RS_CUBE_ON, 1, 1, 0), (FAR, 2, 0, 1), (RS_CUBE_ON, 1, 0, 1), (RS_CUBE_ON, 1, 0, 0), (TERM, 2, 2),
+    (FAR, 2, 0, 0), (FAR, 2, 2, 0), (BACK, 2, 0, 0), (TERM, 2, 3), (INPUT, 1, 1), (BACK, 2, 2, 0), (FAR, 2, 1, 1),
+    (FAR, 2, 1, 0), (BACK, 2, 2, 1), (RS_PLANE, 1, 2, 1), (BACK, 2, 1, 1), (ACT_TURN, 0), (INPUT, 0, 0),
+    (RS_CUBE_ON, 2, 0, 1), (BACK, 2, 0, 1), (BACK, 2, 1, 0), (RS_CUBE_ON, 2, 2, 1), (INPUT, 1, 0),
+    (RS_CUBE_ON, 2, 1, 1), (RS_CUBE_ON, 2, 2, 0), (RS_PLANE, 1, 1, 1), (RS_PLANE, 1, 0, 1), (RS_CUBE_ON, 2, 1, 0),
+    (RS_PLANE, 0, 2, 0), (RS_PLANE, 0, 0, 0), (RS_PLANE_ON, 0, 0), (RS_CUBE_ON, 2, 0, 0), (RS_PLANE, 0, 1, 0),
+    (RS_PLANE_ON, 0, 1), (RS_PLANE_ON, 0, 2), (RS_PLANE, 1, 2, 0), (RS_PLANE_ON, 1, 2), (RS_PLANE, 1, 1, 0),
+    (INPUT, 2, 0), (RS_PLANE, 2, 2, 1), (INPUT, 2, 1), (RS_PLANE, 1, 0, 0), (RS_PLANE, 2, 0, 1), (RS_PLANE, 2, 1, 1),
+    (RS_PLANE, 2, 2, 0), (RS_PLANE_ON, 1, 1), (RS_PLANE_ON, 1, 0), (RS_PLANE, 2, 0, 0), (RS_PLANE, 2, 1, 0),
+    (INPUT, 3, 1), (RS_LINE, 0, 1), (RS_LINE, 0, 2), (RS_LINE, 0, 0), (RS_LINE, 1, 2), (INPUT, 3, 0), (RS_LINE, 1, 1),
+    (RS_LINE, 1, 0), (RS_LINE, 2, 2), (RS_LINE, 2, 1), (RS_LINE, 2, 0), (HIDDEN,), (RS_END, 0, 0), (RS_END, 1, 1),
+    (RS_END, 0, 2), (RS_END, 0, 1), (RS_END, 1, 2), (RS_END, 2, 1), (RS_END, 2, 2), (RS_END, 1, 0), (RS_END, 2, 0),
 )
 
 
@@ -367,31 +367,48 @@
         first, count = columns(g, o)
         add(out_grad.at[pl.ds(g * ROWS, ROWS), pl.ds(first, count)], block(terms, g, o, me), *views)
 
-    def act_turn():
-        act[...] = act_t[...].reshape(GROUPS * units, 2 * half).astype(jnp.float32).T.astype(jnp.bfloat16)
+    def act_turn(which):
+        @pl.when(core == which)
+        def _():
+            act[...] = act_t[...].reshape(GROUPS * units, 2 * half).astype(jnp.float32).T.astype(jnp.bfloat16)
 
     def hidden_turn():
         out_hidden[...] = hid_t[:, :, :, mine].reshape(GROUPS * units, half).T.astype(jnp.bfloat16)
 
-    def input_chunks(i):
-        for k in (2 * i, 2 * i + 1):
-            weight = weights[k // 2, pl.ds(2 * (k % 2), 2)].reshape(GROUPS * units, width)
-            here = columns_of(k, core)
-            stage[k] = jnp.dot(act[theirs, :], weight, preferred_element_type=jnp.float32).astype(jnp.bfloat16)
-            send(stage.at[k], out_input.at[:, here], in_send.at[k], in_recv.at[k], partner)
-            out_input[:, here] = jnp.dot(act[mine, :], weight, preferred_element_type=jnp.float32).astype(jnp.bfloat16)
+    def input_copy(k):
+        return pltpu.make_async_remote_copy(
+            src_ref=stage.at[k], dst_ref=out_input.at[:, columns_of(k, core)], send_sem=in_send.at[k],
+            recv_sem=in_recv.at[k], device_id=partner, device_id_type=MESH,
+        )
+
+    def input_chunks(i, which):
+        @pl.when(core == which)
+        def _():
+            for k in (2 * i, 2 * i + 1):
+                weight = weights[k // 2, pl.ds(2 * (k % 2), 2)].reshape(GROUPS * units, width)
+                stage[k] = jnp.dot(act[theirs, :], weight, preferred_element_type=jnp.float32).astype(jnp.bfloat16)
+                input_copy(k).start()
+                out_input[:, columns_of(k, core)] = jnp.dot(
+                    act[mine, :], weight, preferred_element_type=jnp.float32
+                ).astype(jnp.bfloat16)
 
     steps = (
         ag_line, ag_plane, ag_plane_on, ag_cube, ag_cube_on, tokens_out, tokens_in, cot_turn, forward, partial_out,
         activate, term, rs_far, rs_back, rs_cube_on, rs_plane, rs_plane_on, rs_line, rs_end, act_turn, input_chunks,
         hidden_turn,
     )
+    def drain(keep):
+        while len(sent) > keep:
+            sent.pop(0).wait_send()
+
     for name, *where in SCHEDULE:
+        if name in (RS_PLANE, RS_LINE, RS_END) and where[0] == GROUPS - 1:
+            drain(24)
         steps[name](*where)
     for k in range(8):
         arrived(out_input.at[:, columns_of(k, 1 - core)], in_send.at[k], in_recv.at[k])
-    for copy in sent:
-        copy.wait_send()
+        input_copy(k).wait_send()
+    drain(0)
 
 
 def update(

time: 71.4 us -> 69.3 us (0.971)
  Pallas kernels: 70.4 us -> 68.3 us
    pallas_call x1, Pallas kernels: 67.1 us -> 65 us  [shards(): pl.pallas_call(kernel, out_shape=(pltpu.VMEM((units, width), f32), pltpu....]
where the time goes in v3:
time: 69.3 us; the launch traced here: 69.1 us
  Pallas kernels  68.3 us (99%)
  between operations  0.8 us (1%)
    pallas_call x1, Pallas kernels, shards(): pl.pallas_call(kernel, out_shape=(pltpu.VMEM((units, width), f32), pltpu....  65 us
    pallas_call x1, Pallas kernels, shards(): pl.pallas_call(functools.partial(update, lax.axis_size('node') * lax.axis...  3.36 us

profile of v3, /device:TPU:0, one launch (start us, length us, event | category | flops | bytes accessed | tf_op | source)
XLA Modules:
  0.0 69.1 jit_solution(7117917643265775707)
XLA Ops:
  0.6 65.0 %gather_project_scatter.1 = (f32[48,896]{1,0:T(8,128)S(1)}, bf16[256,384]{1,0:T(8,128)(2,1)S(1)}, bf16[256,14336]{1,0:T(8,128)(2,1)S(1)}) custom-call(f32[48,896]{1,0:T(8,128)} %master.1, bf16[256,14336]{1,0:T(8,128)(2,1)} %tokens.1, bf16[256,384]{1,0:T(8,128)(2,1)} %cot_hbm.1), custom_call_target="tpu_custom_call" | custom-call | tf_op jit(solution)/shard_map/gather_project_scatter/pallas_call | solution.py:463
  65.6 3.4 %adam_and_store.1 = (bf16[256,384]{1,0:T(8,128)(2,1)}, bf16[256,14336]{1,0:T(8,128)(2,1)}, f32[48,896]{1,0:T(8,128)}, f32[48,896]{1,0:T(8,128)}, f32[48,896]{1,0:T(8,128)}, /*index=5*/f32[48,896]{1,0:T(8,128)}) custom-call(f32[48,896]{1,0:T(8,128)S(1)} %get-tuple-element.9.total, bf16[256,384]{1,0:T(8,128)(2,1)S(1)} %get-tuple-element.10.hidden, ...), custom_call_target="tpu_custom_call" | custom-call | tf_op jit(solution)/shard_map/adam_and_store/pallas_call | solution.py:501

commit v4 on v3

--- a/solution.py
+++ b/solution.py
@@ -133,7 +133,6 @@
         own_tokens(i).start()
     own[0].wait()
     weights[me["z"], me["y"], me["x"]] = master[...].astype(jnp.bfloat16)
-    acc[...] = jnp.zeros_like(acc)
     pl.semaphore_wait(barrier, len(around))
 
     sent = []
@@ -229,6 +228,7 @@
             arrived(tok.at[k, theirs, :], tok_send.at[k], tok_recv.at[k])
 
     def cot_turn():
+        acc[...] = jnp.zeros_like(acc)
         own[1].wait()
         arrived(cot.at[1 - core], cot_send, cot_recv)
         turned = cot[...].reshape(2 * half, GROUPS * units).astype(jnp.float32).T
@@ -415,11 +415,6 @@
     blocks, total, hidden, input_grad, master, moment_one, moment_two,
     out_hidden, out_input, out_grad, out_master, out_one, out_two, old, new, in_sem, out_sem,
 ):
-    loads = [
-        pltpu.make_async_copy(value, old.at[i], in_sem.at[i]) for i, value in enumerate((moment_one, moment_two, master))
-    ]
-    for copy in loads:
-        copy.start()
     rows = input_grad.shape[0] // 4
     copies = [
         pltpu.make_async_copy(
@@ -429,6 +424,11 @@
     ]
     copies.append(pltpu.make_async_copy(hidden, out_hidden, out_sem.at[4]))
     for copy in copies:
+        copy.start()
+    loads = [
+        pltpu.make_async_copy(value, old.at[i], in_sem.at[i]) for i, value in enumerate((moment_one, moment_two, master))
+    ]
+    for copy in loads:
         copy.start()
 
     def store(i, value, out):

time: 69.3 us -> 69.3 us (level)
  no operation moved by 1% of the time
where the time goes in v4:
time: 69.3 us; the launch traced here: 69.1 us
  Pallas kernels  68.3 us (99%)
  between operations  0.8 us (1%)
    pallas_call x1, Pallas kernels, shards(): pl.pallas_call(kernel, out_shape=(pltpu.VMEM((units, width), f32), pltpu....  65 us
    pallas_call x1, Pallas kernels, shards(): pl.pallas_call(functools.partial(update, lax.axis_size('node') * lax.axis...  3.36 us

profile of v4, /device:TPU:0, one launch (start us, length us, event | category | flops | bytes accessed | tf_op | source)
XLA Modules:
  0.0 69.1 jit_solution(17765429632109483815)
XLA Ops:
  0.6 65.0 %gather_project_scatter.1 = (f32[48,896]{1,0:T(8,128)S(1)}, bf16[256,384]{1,0:T(8,128)(2,1)S(1)}, bf16[256,14336]{1,0:T(8,128)(2,1)S(1)}) custom-call(f32[48,896]{1,0:T(8,128)} %master.1, bf16[256,14336]{1,0:T(8,128)(2,1)} %tokens.1, bf16[256,384]{1,0:T(8,128)(2,1)} %cot_hbm.1), custom_call_target="tpu_custom_call" | custom-call | tf_op jit(solution)/shard_map/gather_project_scatter/pallas_call | solution.py:463
  65.6 3.4 %adam_and_store.1 = (bf16[256,384]{1,0:T(8,128)(2,1)}, bf16[256,14336]{1,0:T(8,128)(2,1)}, f32[48,896]{1,0:T(8,128)}, f32[48,896]{1,0:T(8,128)}, f32[48,896]{1,0:T(8,128)}, /*index=5*/f32[48,896]{1,0:T(8,128)}) custom-call(f32[48,896]{1,0:T(8,128)S(1)} %get-tuple-element.9.total, bf16[256,384]{1,0:T(8,128)(2,1)S(1)} %get-tuple-element.10.hidden, ...), custom_call_target="tpu_custom_call" | custom-call | tf_op jit(solution)/shard_map/adam_and_store/pallas_call | solution.py:501
